TPU v7x, 32 devices: a whole 2x2x4 slice. The times are simulated.
32 devices in a mesh: groups: 1, ep: 32 (over z, y, x, core).
Axes of the slice: x: 2, y: 2, z: 4, core: 2. Of those that a mesh axis runs over, the one named last changes fastest.
Arguments:
- tokens: bfloat16 [2, 256, 3584], P(None, ('groups', 'ep')), may hold values from -6 to 6
- expert_ids: int32 [2, 256, 8], P(None, ('groups', 'ep')), may hold values from 0 to 15, all different within a row; in each aligned block of 8 rows (0 to 7, 8 to 15, ..., all dimensions but the last counted through in order) at most 8 rows name the same one
- route_weight: float32 [2, 256, 8], P(None, ('groups', 'ep')), may hold values from 0.05 to 1
- gate_weight: bfloat16 [32, 3584, 512], P('ep'), may hold values from -0.09375 to 0.09375
- up_weight: bfloat16 [32, 3584, 512], P('ep'), may hold values from -0.09375 to 0.09375
- down_weight: bfloat16 [32, 512, 3584], P('ep'), may hold values from -0.1875 to 0.1875
Outputs:
- combined: bfloat16 [2, 256, 3584], P(None, ('groups', 'ep'))
Inputs may be any that keep to these rules, and one draw needn't show every extreme that they name: `expert_ids`: each row names 8 different experts; within each step, the 8 rows of one device name any one expert at most 8 times.
All inputs are finite; a program needn't handle non-finite values.
Results may differ from a plain program's by a relative error of at most 0.0065.
Values may be sent and summed in bfloat16 or wider, within the bound.
A program may use at most 64 MiB of HBM per device.

v0:
```python
import jax
import jax.numpy as jnp
from jax import lax
from jax.sharding import PartitionSpec as P

TOP = 8
STEPS = 2


def partner_2(block, axis, apart):
    count = lax.axis_size(axis)
    route = []
    for low in range(count):
        high = low | 1 << apart
        if high != low and high < count:
            route += [(low, high), (high, low)]
    return lax.ppermute(block, axis, route)


def slot_layout(block_ids, expert_count, capacity):
    pairs = block_ids.reshape(-1)
    count = pairs.shape[0]
    one_hot = (pairs[:, None] == jnp.arange(expert_count, dtype=jnp.int32)[None, :]).astype(
        jnp.float32
    )
    order = jnp.arange(count, dtype=jnp.int32)
    earlier = (order[None, :] < order[:, None]).astype(jnp.float32)
    before = jnp.dot(earlier, one_hot, precision=lax.Precision.HIGHEST)
    slot_rank = jnp.sum(before * one_hot, axis=1).astype(jnp.int32)
    slot_index = pairs * capacity + slot_rank
    slot_source = jnp.full((expert_count * capacity,), count, jnp.int32).at[slot_index].set(order)
    return (slot_index, slot_source)


def shards(tokens, expert_ids, route_weight, gate_weight, up_weight, down_weight):
    device_count = lax.axis_size("ep")
    expert_count = device_count // 2
    tok_rows = tokens.shape[1]
    features = tokens.shape[2]
    capacity = min(tok_rows, 2 * tok_rows * TOP // expert_count)
    half_slots = capacity // 2
    gate_m = gate_weight[0]
    up_m = up_weight[0]
    down_m = down_weight[0]
    parity_odd = lax.axis_index("ep") % 2 == 1
    layouts = []
    outgoing = []
    for step_index in range(STEPS):
        slot_index, slot_source = slot_layout(expert_ids[step_index], expert_count, capacity)
        padded = jnp.concatenate(
            [tokens[step_index], jnp.zeros((1, features), tokens.dtype)], axis=0
        )
        blocks = padded[slot_source // TOP].reshape(expert_count, capacity, features)
        arrange_paired = blocks.reshape(expert_count, half_slots, 2, features)
        arrange_paired = jnp.where(parity_odd, arrange_paired[:, :, ::-1], arrange_paired)
        outgoing.append(
            arrange_paired.transpose(0, 2, 1, 3).reshape(device_count, half_slots, features)
        )
        layouts.append(slot_index)
    returned_list = []
    for sent in outgoing:
        received = lax.all_to_all(sent, "ep", split_axis=0, concat_axis=0, tiled=True)
        partner = partner_2(received, "ep", 0)
        width = received.shape[1]
        apply_received = jnp.concatenate([received, partner], axis=1)
        gate = jnp.einsum("scd,df->scf", apply_received, gate_m, preferred_element_type=jnp.float32)
        upper = jnp.einsum("scd,df->scf", apply_received, up_m, preferred_element_type=jnp.float32)
        act = (jax.nn.silu(gate) * upper).astype(jnp.bfloat16)
        parts = jnp.einsum("scf,fd->scd", act, down_m, preferred_element_type=jnp.float32).astype(
            jnp.bfloat16
        )
        back = partner_2(parts[:, width:], "ep", 0)
        summed = (parts[:, :width].astype(jnp.float32) + back.astype(jnp.float32)).astype(
            jnp.bfloat16
        )
        returned_list.append(lax.all_to_all(summed, "ep", split_axis=0, concat_axis=0, tiled=True))
    answers = []
    for step_index in range(STEPS):
        returned = returned_list[step_index]
        paired = returned.reshape(expert_count, 2, half_slots, features).transpose(0, 2, 1, 3)
        paired = jnp.where(parity_odd, paired[:, :, ::-1], paired)
        answers.append(paired.reshape(expert_count, capacity, features))
    outputs = []
    for step_index in range(STEPS):
        flattened = answers[step_index].reshape(expert_count * capacity, features)
        picked = flattened[layouts[step_index]].reshape(tok_rows, TOP, features)
        summed = jnp.sum(route_weight[step_index][:, :, None] * picked.astype(jnp.float32), axis=1)
        outputs.append(summed.astype(jnp.bfloat16))
    return jnp.stack(outputs)


def solution(mesh):
    in_specs = (
        P(None, ("groups", "ep"), None),
        P(None, ("groups", "ep"), None),
        P(None, ("groups", "ep"), None),
        P("ep", None, None),
        P("ep", None, None),
        P("ep", None, None),
    )
    out_specs = P(None, ("groups", "ep"), None)
    return jax.shard_map(shards, mesh=mesh, in_specs=in_specs, out_specs=out_specs, check_vma=False)
```

profile of v0, /device:TPU:0, one launch (start us, length us, event | category | flops | bytes accessed | tf_op | source)
XLA Modules:
  0.0 149.8 jit_solution(7503540758091043360)
XLA Ops:
  1.9 0.9 slice_bitcast_fusion.1
  2.7 1.1 gather_fusion
  4.6 1.3 reverse_select_fusion.3
  5.9 7.3 %all-to-all-start = ((bf16[32,4,3584]{2,1,0:T(4,128)(2,1)}), bf16[32,4,3584]{2,1,0:T(4,128)(2,1)S(1)}, u32[]{:S(2)}, u32[]{:S(2)}) async-start(bf16[32,4,3584]{2,1,0:T(4,128)(2,1)} %bitcast.5), calls=%async_computation | async-start | bytes 1835008 | tf_op jit(solution)/shard_map/all_to_all | solution.py:62
  14.4 1.1 gather_fusion.2
  16.2 1.3 reverse_select_fusion.1
  17.5 19.1 %all-to-all-done = bf16[32,4,3584]{2,1,0:T(4,128)(2,1)S(1)} async-done(((bf16[32,4,3584]{2,1,0:T(4,128)(2,1)}), bf16[32,4,3584]{2,1,0:T(4,128)(2,1)S(1)}, u32[]{:S(2)}, u32[]{:S(2)}) %all-to-all-start) | async-done | bytes 917536 | tf_op jit(solution)/shard_map/all_to_all | solution.py:62
  36.6 3.9 %all-to-all-start.2 = ((bf16[32,4,3584]{2,1,0:T(4,128)(2,1)}), bf16[32,4,3584]{2,1,0:T(4,128)(2,1)}, u32[]{:S(2)}, u32[]{:S(2)}) async-start(bf16[32,4,3584]{2,1,0:T(4,128)(2,1)} %bitcast.21), calls=%async_computation.2 | async-start | bytes 1835008 | tf_op jit(solution)/shard_map/all_to_all | solution.py:62
  40.6 23.2 %all-to-all-done.2 = bf16[32,4,3584]{2,1,0:T(4,128)(2,1)} async-done(((bf16[32,4,3584]{2,1,0:T(4,128)(2,1)}), bf16[32,4,3584]{2,1,0:T(4,128)(2,1)}, u32[]{:S(2)}, u32[]{:S(2)}) %all-to-all-start.2) | async-done | bytes 917536 | tf_op jit(solution)/shard_map/all_to_all | solution.py:62
  63.8 0.9 copy-done.1
  64.7 3.2 %fusion.4 = f32[32,8,512]{2,1,0:T(8,128)S(1)} fusion(bf16[1,3584,512]{2,1,0:T(8,128)(2,1)} %param.10, bf16[32,4,3584]{2,1,0:T(4,128)(2,1)S(1)} %collective-permute-done, bf16[32,4,3584]{2,1,0:T(4,128)(2,1)S(1)} %all-to-all-done), kind=kOutput, calls=%fused_computation.12 | convolution fusion | flops 943194112 | bytes 6029312 | tf_op jit(solution)/shard_map/scd,df->scf/dot_general | solution.py:67
  67.9 5.7 %convolution_convert_fusion.1 = bf16[32,8,3584]{2,1,0:T(8,128)(2,1)S(1)} fusion(bf16[1,512,3584]{2,1,0:T(8,128)(2,1)} %param.11, f32[32,8,512]{2,1,0:T(8,128)S(1)} %fusion.4, bf16[1,3584,512]{2,1,0:T(8,128)(2,1)} %param.9, bf16[32,4,3584]{2,1,0:T(4,128)(2,1)} %copy-done.1, bf16[32,4,3584]{2,1,0:T(4,128)(2,1)S(1)} %all-to-all-done), kind=kOutput, calls=%fused_computation.7 | convolution fusion | flops 1884422144 | bytes 11534336 | tf_op jit(solution)/shard_map/scf,fd->scd/dot_general | solution.py:69
  74.6 3.7 %fusion.2 = f32[32,8,512]{2,1,0:T(8,128)S(1)} fusion(bf16[1,3584,512]{2,1,0:T(8,128)(2,1)} %param.10, bf16[32,4,3584]{2,1,0:T(4,128)(2,1)} %collective-permute-done.2, bf16[32,4,3584]{2,1,0:T(4,128)(2,1)} %all-to-all-done.2), kind=kOutput, calls=%fused_computation.10 | convolution fusion | flops 943194112 | bytes 6029312 | tf_op jit(solution)/shard_map/scd,df->scf/dot_general | solution.py:67
  78.3 7.2 %convolution_convert_fusion = bf16[32,8,3584]{2,1,0:T(8,128)(2,1)} fusion(bf16[1,512,3584]{2,1,0:T(8,128)(2,1)} %param.11, f32[32,8,512]{2,1,0:T(8,128)S(1)} %fusion.2, bf16[1,3584,512]{2,1,0:T(8,128)(2,1)} %param.9, bf16[32,4,3584]{2,1,0:T(4,128)(2,1)} %collective-permute-done.2, bf16[32,4,3584]{2,1,0:T(4,128)(2,1)} %all-to-all-done.2), kind=kOutput, calls=%fused_computation.6 | convolution fusion | flops 1884422144 | bytes 11534336 | tf_op jit(solution)/shard_map/scf,fd->scd/dot_general | solution.py:69
  85.5 2.9 %slice.51 = bf16[32,4,3584]{2,1,0:T(4,128)(2,1)} slice(bf16[32,8,3584]{2,1,0:T(8,128)(2,1)} %convolution_convert_fusion), slice={[0:32], [4:8], [0:3584]} | slice | bytes 1835008 | tf_op jit(solution)/shard_map/slice | solution.py:72
  88.4 2.6 %add_convert_fusion.1 = bf16[32,4,3584]{2,1,0:T(4,128)(2,1)} fusion(bf16[32,4,3584]{2,1,0:T(4,128)(2,1)} %collective-permute-done.1, bf16[32,8,3584]{2,1,0:T(8,128)(2,1)S(1)} %convolution_convert_fusion.1), kind=kLoop, calls=%fused_computation.21 | loop fusion | flops 1835008 | bytes 2752512 | tf_op jit(solution)/shard_map/convert_element_type | solution.py:73
  91.1 3.7 %all-to-all-start.1 = ((bf16[32,4,3584]{2,1,0:T(4,128)(2,1)}), bf16[32,4,3584]{2,1,0:T(4,128)(2,1)S(1)}, u32[]{:S(2)}, u32[]{:S(2)}) async-start(bf16[32,4,3584]{2,1,0:T(4,128)(2,1)} %add_convert_fusion.1), calls=%async_computation.1 | async-start | bytes 1835008 | tf_op jit(solution)/shard_map/all_to_all | solution.py:76
  94.8 3.2 %add_convert_fusion = bf16[32,4,3584]{2,1,0:T(4,128)(2,1)} fusion(bf16[32,4,3584]{2,1,0:T(4,128)(2,1)} %collective-permute-done.3, bf16[32,8,3584]{2,1,0:T(8,128)(2,1)} %convolution_convert_fusion), kind=kLoop, calls=%fused_computation.20 | loop fusion | flops 1835008 | bytes 2752512 | tf_op jit(solution)/shard_map/convert_element_type | solution.py:73
  98.0 20.2 %all-to-all-done.1 = bf16[32,4,3584]{2,1,0:T(4,128)(2,1)S(1)} async-done(((bf16[32,4,3584]{2,1,0:T(4,128)(2,1)}), bf16[32,4,3584]{2,1,0:T(4,128)(2,1)S(1)}, u32[]{:S(2)}, u32[]{:S(2)}) %all-to-all-start.1) | async-done | bytes 917536 | tf_op jit(solution)/shard_map/all_to_all | solution.py:76
  118.2 3.8 %all-to-all-start.3 = ((bf16[32,4,3584]{2,1,0:T(4,128)(2,1)}), bf16[32,4,3584]{2,1,0:T(4,128)(2,1)S(1)}, u32[]{:S(2)}, u32[]{:S(2)}) async-start(bf16[32,4,3584]{2,1,0:T(4,128)(2,1)} %add_convert_fusion), calls=%async_computation.3 | async-start | bytes 1835008 | tf_op jit(solution)/shard_map/all_to_all | solution.py:76
  123.6 21.7 %all-to-all-done.3 = bf16[32,4,3584]{2,1,0:T(4,128)(2,1)S(1)} async-done(((bf16[32,4,3584]{2,1,0:T(4,128)(2,1)}), bf16[32,4,3584]{2,1,0:T(4,128)(2,1)S(1)}, u32[]{:S(2)}, u32[]{:S(2)}) %all-to-all-start.3) | async-done | bytes 917536 | tf_op jit(solution)/shard_map/all_to_all | solution.py:76
  146.7 0.8 gather_fusion.1
  147.5 0.8 gather_fusion.3
  148.4 0.8 fusion.12
  (45 shorter events, 9.0 us)
Async XLA Ops:
  5.9 30.7 %all-to-all-start = ((bf16[32,4,3584]{2,1,0:T(4,128)(2,1)}), bf16[32,4,3584]{2,1,0:T(4,128)(2,1)S(1)}, u32[]{:S(2)}, u32[]{:S(2)}) async-start(bf16[32,4,3584]{2,1,0:T(4,128)(2,1)} %bitcast.5), calls=%async_computation | async-start | bytes 1835008 | tf_op jit(solution)/shard_map/all_to_all | solution.py:62
  36.6 27.2 %all-to-all-start.2 = ((bf16[32,4,3584]{2,1,0:T(4,128)(2,1)}), bf16[32,4,3584]{2,1,0:T(4,128)(2,1)}, u32[]{:S(2)}, u32[]{:S(2)}) async-start(bf16[32,4,3584]{2,1,0:T(4,128)(2,1)} %bitcast.21), calls=%async_computation.2 | async-start | bytes 1835008 | tf_op jit(solution)/shard_map/all_to_all | solution.py:62
  40.5 23.2 %collective-permute-start = (bf16[32,4,3584]{2,1,0:T(4,128)(2,1)S(1)}, bf16[32,4,3584]{2,1,0:T(4,128)(2,1)S(1)}, u32[]{:S(2)}, u32[]{:S(2)}) collective-permute-start(bf16[32,4,3584]{2,1,0:T(4,128)(2,1)S(1)} %all-to-all-done), channel_id=1, source_target_pairs={{0,1},{1,0},{2,3},{3,2},{4,5},{5,4},{6,7},{7,6},{8,9},{9,8},{10,11... | collective-permute-start | bytes 2752520 | tf_op jit(solution)/shard_map/ppermute | solution.py:17
  63.8 10.8 %collective-permute-start.2 = (bf16[32,4,3584]{2,1,0:T(4,128)(2,1)}, bf16[32,4,3584]{2,1,0:T(4,128)(2,1)}, u32[]{:S(2)}, u32[]{:S(2)}) collective-permute-start(bf16[32,4,3584]{2,1,0:T(4,128)(2,1)} %all-to-all-done.2), channel_id=1, source_target_pairs={{0,1},{1,0},{2,3},{3,2},{4,5},{5,4},{6,7},{7,6},{8,9},{9,8},{10,11... | collective-permute-start | bytes 2752520 | tf_op jit(solution)/shard_map/ppermute | solution.py:17
  63.8 0.9 copy-start.1
  74.0 14.4 %collective-permute-start.1 = (bf16[32,4,3584]{2,1,0:T(4,128)(2,1)S(1)}, bf16[32,4,3584]{2,1,0:T(4,128)(2,1)}, u32[]{:S(2)}, u32[]{:S(2)}) collective-permute-start(bf16[32,4,3584]{2,1,0:T(4,128)(2,1)S(1)} %slice.49), channel_id=1, source_target_pairs={{0,1},{1,0},{2,3},{3,2},{4,5},{5,4},{6,7},{7,6},{8,9},{9,8},{10,11... | collective-permute-start | bytes 2752520 | tf_op jit(solution)/shard_map/ppermute | solution.py:17
  88.4 6.4 %collective-permute-start.3 = (bf16[32,4,3584]{2,1,0:T(4,128)(2,1)}, bf16[32,4,3584]{2,1,0:T(4,128)(2,1)}, u32[]{:S(2)}, u32[]{:S(2)}) collective-permute-start(bf16[32,4,3584]{2,1,0:T(4,128)(2,1)} %slice.51), channel_id=1, source_target_pairs={{0,1},{1,0},{2,3},{3,2},{4,5},{5,4},{6,7},{7,6},{8,9},{9,8},{10,11... | collective-permute-start | bytes 2752520 | tf_op jit(solution)/shard_map/ppermute | solution.py:17
  91.1 31.0 %copy-start = (f32[2,8,8]{2,1,0:T(8,128)S(1)}, f32[2,8,8]{2,1,0:T(8,128)}, u32[]{:S(2)}) copy-start(f32[2,8,8]{2,1,0:T(8,128)} %param.8) | copy-start | bytes 1540
  91.1 27.1 %all-to-all-start.1 = ((bf16[32,4,3584]{2,1,0:T(4,128)(2,1)}), bf16[32,4,3584]{2,1,0:T(4,128)(2,1)S(1)}, u32[]{:S(2)}, u32[]{:S(2)}) async-start(bf16[32,4,3584]{2,1,0:T(4,128)(2,1)} %add_convert_fusion.1), calls=%async_computation.1 | async-start | bytes 1835008 | tf_op jit(solution)/shard_map/all_to_all | solution.py:76
  118.2 27.1 %all-to-all-start.3 = ((bf16[32,4,3584]{2,1,0:T(4,128)(2,1)}), bf16[32,4,3584]{2,1,0:T(4,128)(2,1)S(1)}, u32[]{:S(2)}, u32[]{:S(2)}) async-start(bf16[32,4,3584]{2,1,0:T(4,128)(2,1)} %add_convert_fusion), calls=%async_computation.3 | async-start | bytes 1835008 | tf_op jit(solution)/shard_map/all_to_all | solution.py:76
where the time goes:
time: 151 us; the launch traced here: 150 us
  waiting for transfers between devices  84.2 us (56%)
  matrix products  20 us (13%)
  starting transfers between devices  19.4 us (13%)
  local copies, waits for them, and re-layouts  14.5 us (10%)
  other arithmetic  11.4 us (8%)
    all_to_all x2, waiting for transfers between devices, shards(): lax.all_to_all(sent, 'ep', split_axis=0, concat_axis=0, tiled=True)  42.3 us
    all_to_all x2, waiting for transfers between devices, shards(): lax.all_to_all(summed, 'ep', split_axis=0, concat_axis=0, tiled=True)  41.9 us
    dot_general x2, matrix products, shards(): jnp.einsum('scf,fd->scd', act, down_m, preferred_element_type=jnp.float32)  12.8 us
    all_to_all x2, starting transfers between devices, shards(): lax.all_to_all(sent, 'ep', split_axis=0, concat_axis=0, tiled=True)  11.2 us
    all_to_all x2, starting transfers between devices, shards(): lax.all_to_all(summed, 'ep', split_axis=0, concat_axis=0, tiled=True)  7.55 us
    dot_general x2, matrix products, shards(): jnp.einsum('scd,df->scf', apply_received, up_m, preferred_element_type=jn...  6.87 us
    convert_element_type x2, other arithmetic, shards(): (parts[:, :width].astype(jnp.float32) + back.astype(jnp.float32)).astype(...  5.83 us
    slice x2, local copies, waits for them, and re-layouts, shards(): back = partner_2(parts[:, width:], 'ep', 0)  3.38 us
  transfers between devices with their start and end apart: 8, of which 4 were waited for; matrix products, arithmetic and copies ran while one was open for 23% of the time, Pallas kernels for 0%

commit v1 on v0

--- a/solution.py
+++ b/solution.py
@@ -32,12 +32,28 @@
     return (slot_index, slot_source)
 
 
+def dense(tokens, expert_ids, route_weight, gate_weight, up_weight, down_weight):
+    expert_count = lax.axis_size("ep") // 2
+    named = expert_ids[..., None] == jnp.arange(expert_count, dtype=jnp.int32)
+    coef = jnp.sum(jnp.where(named, route_weight[..., None], 0.0), axis=2)
+    coefs = lax.all_gather(coef, "ep", axis=1, tiled=True)
+    rows = lax.all_gather(tokens, "ep", axis=1, tiled=True)
+    mine = lax.dynamic_index_in_dim(coefs, lax.axis_index("ep") // 2, axis=2, keepdims=True)
+    gate = jnp.einsum("std,df->stf", rows, gate_weight[0], preferred_element_type=jnp.float32)
+    upper = jnp.einsum("std,df->stf", rows, up_weight[0], preferred_element_type=jnp.float32)
+    act = (mine * (jax.nn.silu(gate) * upper)).astype(jnp.bfloat16)
+    part = jnp.einsum("stf,fd->std", act, down_weight[0], preferred_element_type=jnp.float32)
+    return lax.psum_scatter(part.astype(jnp.bfloat16), "ep", scatter_dimension=1, tiled=True)
+
+
 def shards(tokens, expert_ids, route_weight, gate_weight, up_weight, down_weight):
     device_count = lax.axis_size("ep")
     expert_count = device_count // 2
     tok_rows = tokens.shape[1]
     features = tokens.shape[2]
     capacity = min(tok_rows, 2 * tok_rows * TOP // expert_count)
+    if capacity == tok_rows:
+        return dense(tokens, expert_ids, route_weight, gate_weight, up_weight, down_weight)
     half_slots = capacity // 2
     gate_m = gate_weight[0]
     up_m = up_weight[0]

time: 151 us -> 244 us (1.62)
  waiting for transfers between devices: 84.2 us -> 160 us
  blocking collectives: 0 us -> 44.2 us
  starting transfers between devices: 19.4 us -> 0.04 us
  between operations: 0.3 us -> 13.4 us
  other arithmetic: 11.4 us -> 0.82 us
  matrix products: 20 us -> 15.3 us
  local copies, waits for them, and re-layouts: 14.5 us -> 10.2 us
    unnamed x0 -> x3, waiting for transfers between devices: none -> 139 us
    all_to_all x4 -> x0, waiting for transfers between devices: 84.2 us -> none  [the longest x2 42.3 us: shards(): lax.all_to_all(sent, 'ep', split_axis=0, concat_axis=0, tiled=True)]
    all_gather x0 -> x1, blocking collectives: none -> 44.2 us  [dense(): coefs = lax.all_gather(coef, 'ep', axis=1, tiled=True)]
    all_gather x0 -> x1, waiting for transfers between devices: none -> 21 us  [dense(): rows = lax.all_gather(tokens, 'ep', axis=1, tiled=True)]
    all_to_all x4 -> x0, starting transfers between devices: 18.8 us -> none  [the longest x2 11.2 us: shards(): lax.all_to_all(sent, 'ep', split_axis=0, concat_axis=0, tiled=True)]
    unnamed x4, local copies, waits for them, and re-layouts: 0.95 us -> 9.74 us
    convert_element_type x2 -> x0, other arithmetic: 5.83 us -> none  [shards(): (parts[:, :width].astype(jnp.float32) + back.astype(jnp.float32)).astype(...]
    dot_general x6 -> x2, matrix products: 20 us -> 15.3 us  [the longest x1 10.1 us: dense(): jnp.einsum('stf,fd->std', act, down_weight[0], preferred_element_type=jnp...]
  transfers between devices with their start and end apart: 8 -> 2, of which waited for: 4 -> 2; matrix products, arithmetic and copies ran while one was open for 23% -> 1% of each run, Pallas kernels for 0% -> 0%
where the time goes in v1:
time: 244 us
  waiting for transfers between devices  160 us (66%)
  blocking collectives  44.2 us (18%)
  matrix products  15.3 us (6%)
  between operations  13.4 us (5%)
  local copies, waits for them, and re-layouts  10.2 us (4%)
    unnamed x3, waiting for transfers between devices  139 us
    all_gather x1, blocking collectives, dense(): coefs = lax.all_gather(coef, 'ep', axis=1, tiled=True)  44.2 us
    all_gather x1, waiting for transfers between devices, dense(): rows = lax.all_gather(tokens, 'ep', axis=1, tiled=True)  21 us
    dot_general x1, matrix products, dense(): jnp.einsum('stf,fd->std', act, down_weight[0], preferred_element_type=jnp...  10.1 us
    unnamed x4, local copies, waits for them, and re-layouts  9.74 us
    dot_general x1, matrix products, dense(): jnp.einsum('std,df->stf', rows, gate_weight[0], preferred_element_type=jn...  5.21 us
  transfers between devices with their start and end apart: 2, of which 2 were waited for; matrix products, arithmetic and copies ran while one was open for 1% of the time, Pallas kernels for 0%

profile of v1, /device:TPU:0, one launch (start us, length us, event | category | flops | bytes accessed | tf_op | source)
XLA Modules:
  0.0 244.1 jit_solution(11328468200609107425)
XLA Ops:
  6.5 0.0 all-gather.2.cloned.1.call-start
  6.5 0.7 all-gather.2.cloned.1.call-update
  7.3 0.0 reduce-scatter.4.cloned.1.call-start
  7.3 0.8 select_reduce_fusion
  8.2 44.2 %all_gather.6 = f32[2,256,16]{2,0,1:T(2,128)S(1)} all-gather(f32[2,8,16]{2,0,1:T(2,128)S(1)} %copy.8), channel_id=1, replica_groups=mesh['groups'=1,'ep'=32] {'ep'}, dimensions={1}, use_global_device_ids=true | all-gather | bytes 33792 | tf_op jit(solution)/shard_map/all_gather | solution.py:39
  52.4 0.3 constant_dynamic-slice_fusion
  52.7 0.1 copy.9
  52.8 21.0 %all-gather.2.cloned.1.call-done = bf16[2,256,3584]{2,1,0:T(8,128)(2,1)} async-done(((bf16[2,8,3584]{2,1,0:T(8,128)(2,1)}), bf16[2,256,3584]{2,1,0:T(8,128)(2,1)}) %all-gather.2.cloned.1.call-update) | async-done | bytes 3670032 | tf_op jit(solution)/shard_map/all_gather | solution.py:40
  73.8 5.2 %fusion.3 = f32[2,256,512]{2,1,0:T(8,128)S(1)} fusion(bf16[2,256,3584]{2,1,0:T(8,128)(2,1)} %all-gather.2.cloned.1.call-done, bf16[1,3584,512]{2,1,0:T(8,128)(2,1)} %param.9), kind=kOutput, calls=%fused_computation.4 | convolution fusion | flops 1879048192 | bytes 8388608 | tf_op jit(solution)/shard_map/std,df->stf/dot_general | solution.py:42
  79.0 10.1 %convolution_convert_fusion = bf16[2,256,3584]{2,1,0:T(8,128)(2,1)} fusion(bf16[1,512,3584]{2,1,0:T(8,128)(2,1)} %param.11, bf16[2,256,3584]{2,1,0:T(8,128)(2,1)} %all-gather.2.cloned.1.call-done, bf16[1,3584,512]{2,1,0:T(8,128)(2,1)} %param.10, f32[2,256,512]{2,1,0:T(8,128)S(1)} %fusion.3, f32[2,256]{1,0:T(2,128)S(1)} %bitcast.30), kind=kOutput, calls=%fused_computation | convolution fusion | flops 3761766400 | bytes 15730688 | tf_op jit(solution)/shard_map/stf,fd->std/dot_general | solution.py:45
  89.2 5.8 %copy.10 = bf16[2,256,3584]{2,0,1:T(2,128)(2,1)S(1)} copy(bf16[2,256,3584]{2,1,0:T(8,128)(2,1)} %convolution_convert_fusion) | data formatting | bytes 7340032
  95.0 2.3 copy.12
  97.3 0.0 reduce-scatter.4.cloned.1.call-update
  97.3 138.4 %reduce-scatter.4.cloned.1.call-done = bf16[8,7168]{1,0:T(8,128)(2,1)} async-done(((bf16[256,7168]{1,0:T(8,128)(2,1)}), bf16[8,7168]{1,0:T(8,128)(2,1)}) %reduce-scatter.4.cloned.1.call-update) | async-done | bytes 114704
  235.7 1.0 reshape.6
  236.6 0.7 copy.11
  (1 shorter events, 0.0 us)
Async XLA Ops:
  6.5 67.3 %all-gather.2.cloned.1.call-start = ((), (), s32[]{:S(2)}) async-start(), calls=%async_computation.1 | async-start | bytes 3784704 | tf_op jit(solution)/shard_map/all_gather | solution.py:40
  7.3 228.4 %reduce-scatter.4.cloned.1.call-start = ((), (), s32[]{:S(2)}) async-start(), calls=%async_computation.2 | async-start | bytes 3784704
Sparse Core Ops, SparseCore 0:
  10.2 63.5 all-gather.1
  97.4 138.1 reduce-scatter.3

commit v2 on v0

--- a/solution.py
+++ b/solution.py
@@ -1,6 +1,10 @@
+import functools
+
 import jax
 import jax.numpy as jnp
 from jax import lax
+from jax.experimental import pallas as pl
+from jax.experimental.pallas import tpu as pltpu
 from jax.sharding import PartitionSpec as P
 
 TOP = 8
@@ -32,12 +36,306 @@
     return (slot_index, slot_source)
 
 
+LANES = 128
+SQUARE = 4
+CORES = 2
+FF_TILE = 256
+OUT_TILE = 512
+
+
+def peer_at(k, z, nz):
+    low = lax.div(2 * (nz - 1 - z) + 1, nz)
+    at = z * low + (nz - 1 - z) * (1 - low)
+    other = k + lax.div(k - at + nz, nz)
+    return other * low + (nz - 1 - other) * (1 - low)
+
+
+def fused_kernel(
+    nz, tok_ref, ids_ref, route_ref, gate_hbm, up_hbm, down_hbm, out_ref,
+    gate_w, up_w, down_w, xg, act, part, rs, r1, r2, rz,
+    w_sem, x_recv, x_send_z, x_send_a, x_send_b, x_send_s,
+    rs_send, rs_recv, r1_send, r1_recv, r2_send, r2_recv, rz_send, rz_recv,
+):
+    steps, tok_rows, features = tok_ref.shape
+    rows = steps * tok_rows
+    hidden = act.shape[1]
+    experts = nz * SQUARE
+    me = lax.axis_index("ep")
+    c = lax.rem(me, CORES)
+    expert = lax.div(me, CORES)
+    q = lax.rem(expert, SQUARE)
+    z = lax.div(expert, SQUARE)
+    x, y = lax.rem(q, 2), lax.div(q, 2)
+    qx, qy = 2 * y + 1 - x, 2 * (1 - y) + x
+    qa = qx * (1 - c) + qy * c
+    qb = qy * (1 - c) + qx * c
+    qd = 3 - q
+    s = 1 - c
+
+    def device(to_z, to_q, to_c):
+        return {"ep": (to_z * SQUARE + to_q) * CORES + to_c}
+
+    sibling, along_a, along_b = device(z, q, s), device(z, qa, c), device(z, qb, c)
+    peers = [peer_at(k, z, nz) for k in range(nz - 1)]
+    near = [z] + peers
+
+    loads = [
+        pltpu.make_async_copy(gate_hbm.at[0], gate_w, w_sem.at[0]),
+        pltpu.make_async_copy(up_hbm.at[0], up_w, w_sem.at[1]),
+        pltpu.make_async_copy(down_hbm.at[0], down_w, w_sem.at[2]),
+    ]
+    barrier = pltpu.get_barrier_semaphore()
+    partners = [device(p, q, c) for p in peers] + [along_a, along_b, sibling]
+    for partner in partners:
+        pl.semaphore_signal(
+            barrier, inc=1, device_id=partner, device_id_type=pl.DeviceIdType.MESH
+        )
+    for load in loads:
+        load.start()
+
+    xg[q, c, z, :, :features] = (
+        tok_ref[...].astype(jnp.float32).reshape(rows, features).astype(jnp.bfloat16)
+    )
+    lane = lax.broadcasted_iota(jnp.int32, (rows, LANES), 1)
+    lane_expert, lane_piece = lax.rem(lane, experts), lax.div(lane, experts)
+    ids = ids_ref[...].reshape(rows, TOP)
+    route = route_ref[...].reshape(rows, TOP)
+    coef = jnp.zeros((rows, LANES), jnp.float32)
+    for k in range(TOP):
+        coef += jnp.where(ids[:, k : k + 1] == lane_expert, route[:, k : k + 1], 0.0)
+    high = coef.astype(jnp.bfloat16).astype(jnp.float32)
+    middle = (coef - high).astype(jnp.bfloat16).astype(jnp.float32)
+    low = coef - high - middle
+    pieces = jnp.where(
+        lane_piece == 0,
+        high,
+        jnp.where(lane_piece == 1, middle, jnp.where(lane_piece == 2, low, 0.0)),
+    )
+    xg[q, c, z, :, features:] = pieces.astype(jnp.bfloat16)
+    pl.semaphore_wait(barrier, len(partners))
+
+    sends = []
+
+    def send(src, dst, send_sem, recv_sem, to):
+        copy = pltpu.make_async_remote_copy(
+            src_ref=src,
+            dst_ref=dst,
+            send_sem=send_sem,
+            recv_sem=recv_sem,
+            device_id=to,
+            device_id_type=pl.DeviceIdType.MESH,
+        )
+        copy.start()
+        sends.append(copy)
+
+    def arrived(dst, recv_sem):
+        pltpu.make_async_remote_copy(
+            src_ref=dst,
+            dst_ref=dst,
+            send_sem=x_send_s.at[0, 0],
+            recv_sem=recv_sem,
+            device_id=sibling,
+            device_id_type=pl.DeviceIdType.MESH,
+        ).wait_recv()
+
+    def send_rows(at, send_sem, to):
+        send(xg.at[at], xg.at[at], send_sem, x_recv.at[at], to)
+
+    def rows_arrived(at):
+        arrived(xg.at[at], x_recv.at[at])
+
+    def forward_a(k):
+        at = (qa, c, near[k])
+        rows_arrived(at)
+        send_rows(at, x_send_b.at[1, k], along_b)
+        send_rows(at, x_send_s.at[1, k], sibling)
+
+    for k in range(nz - 1):
+        send_rows((q, c, z), x_send_z.at[k], device(peers[k], q, c))
+    send_rows((q, c, z), x_send_a.at[0], along_a)
+    send_rows((q, c, z), x_send_b.at[0, 0], along_b)
+    send_rows((q, c, z), x_send_s.at[0, 0], sibling)
+    for k in range(1, nz):
+        at = (q, c, near[k])
+        rows_arrived(at)
+        send_rows(at, x_send_a.at[k], along_a)
+        send_rows(at, x_send_b.at[0, k], along_b)
+        send_rows(at, x_send_s.at[0, k], sibling)
+        forward_a(k - 1)
+    forward_a(nz - 1)
+
+    def experts_on(blocks):
+        def gathered():
+            return jnp.concatenate(
+                [xg[bq, bc, :, :, :features].reshape(nz * rows, features) for bq, bc in blocks],
+                axis=0,
+            )
+
+        tail = jnp.concatenate(
+            [xg[bq, bc, :, :, features:].reshape(nz * rows, LANES) for bq, bc in blocks], axis=0
+        ).astype(jnp.float32)
+        tail_lane = lax.broadcasted_iota(jnp.int32, tail.shape, 1)
+        scale = jnp.sum(
+            jnp.where(lax.rem(tail_lane, experts) == expert, tail, 0.0), axis=1, keepdims=True
+        )
+
+        def hidden_tile(j, carry):
+            columns = pl.ds(pl.multiple_of(j * FF_TILE, FF_TILE), FF_TILE)
+            gate = jnp.dot(gathered(), gate_w[:, columns], preferred_element_type=jnp.float32)
+            upper = jnp.dot(gathered(), up_w[:, columns], preferred_element_type=jnp.float32)
+            silu = gate / (1.0 + jnp.exp(-gate))
+            act[:, columns] = (scale * (silu * upper)).astype(jnp.bfloat16)
+            return carry
+
+        def out_tile(j, carry):
+            columns = pl.ds(pl.multiple_of(j * OUT_TILE, OUT_TILE), OUT_TILE)
+            result = jnp.dot(
+                act[...], down_w[:, columns], preferred_element_type=jnp.float32
+            ).astype(jnp.bfloat16)
+            for number, (bq, bc) in enumerate(blocks):
+                part[bq, bc, :, :, columns] = result[
+                    number * nz * rows : (number + 1) * nz * rows
+                ].reshape(nz, rows, OUT_TILE)
+            return carry
+
+        lax.fori_loop(0, hidden // FF_TILE, hidden_tile, 0)
+        lax.fori_loop(0, features // OUT_TILE, out_tile, 0)
+
+    def f32(ref, *at):
+        return ref[at].astype(jnp.float32)
+
+    def send_half(at):
+        send(part.at[at, s], rs.at[at], rs_send.at[at], rs_recv.at[at], sibling)
+
+    def half_arrived(at):
+        arrived(rs.at[at], rs_recv.at[at])
+
+    for k in range(nz):
+        rows_arrived((q, s, near[k]))
+        rows_arrived((qb, s, near[k]))
+    for load in loads:
+        load.wait()
+    experts_on([(q, c), (q, s), (qa, c), (qb, s)])
+    send_half(q)
+    send_half(qb)
+    for k in range(nz):
+        for number, at in ((2, (qb, c, near[k])), (3, (qd, c, near[k]))):
+            rows_arrived(at)
+            send_rows(at, x_send_s.at[number, k], sibling)
+
+    far = [near[k] for k in range(nz - 1, -1, -1)]
+    half_arrived(q)
+    half_arrived(qa)
+    for k in range(nz):
+        at = far[k]
+        part[qa, c, at] = (f32(part, qa, c, at) + f32(rs, qa, at)).astype(jnp.bfloat16)
+        send(part.at[qa, c, at], r1.at[0, at], r1_send.at[0, k], r1_recv.at[0, at], along_a)
+
+    for k in range(nz):
+        rows_arrived((qa, s, near[k]))
+        rows_arrived((qd, s, near[k]))
+    experts_on([(qd, c), (qd, s), (qb, c), (qa, s)])
+    send_half(qd)
+    send_half(qa)
+    half_arrived(qd)
+    for k in range(nz):
+        at = far[k]
+        part[qd, c, at] = (f32(part, qd, c, at) + f32(rs, qd, at)).astype(jnp.bfloat16)
+        send(part.at[qd, c, at], r1.at[1, at], r1_send.at[1, k], r1_recv.at[1, at], along_a)
+    half_arrived(qb)
+
+    def sum_b(k):
+        at = far[k]
+        arrived(r1.at[1, at], r1_recv.at[1, at])
+        part[qb, c, at] = (
+            f32(part, qb, c, at) + f32(rs, qb, at) + f32(r1, 1, at)
+        ).astype(jnp.bfloat16)
+        send(part.at[qb, c, at], r2.at[at], r2_send.at[k], r2_recv.at[at], along_b)
+
+    def sum_own(k):
+        at = far[k]
+        arrived(r1.at[0, at], r1_recv.at[0, at])
+        arrived(r2.at[at], r2_recv.at[at])
+        return f32(part, q, c, at) + f32(rs, q, at) + f32(r1, 0, at) + f32(r2, at)
+
+    sum_b(0)
+    for k in range(nz - 1):
+        sum_b(k + 1)
+        at = far[k]
+        part[q, c, at] = sum_own(k).astype(jnp.bfloat16)
+        send(part.at[q, c, at], rz.at[z], rz_send.at[k], rz_recv.at[z], device(at, q, c))
+    total = sum_own(nz - 1)
+    for peer in peers:
+        arrived(rz.at[peer], rz_recv.at[peer])
+        total += f32(rz, peer)
+    out_ref[...] = total.reshape(steps, tok_rows, features).astype(out_ref.dtype)
+    for copy in sends:
+        copy.wait_send()
+
+
+def fused(tokens, expert_ids, route_weight, gate_weight, up_weight, down_weight):
+    device_count = lax.axis_size("ep")
+    nz = device_count // (SQUARE * CORES)
+    steps, tok_rows, features = tokens.shape
+    hidden = gate_weight.shape[2]
+    rows = steps * tok_rows
+    group = nz * rows
+    kind = tokens.dtype
+    dma = pltpu.SemaphoreType.DMA
+    vmem = pl.BlockSpec(memory_space=pltpu.VMEM)
+    hbm = pl.BlockSpec(memory_space=pl.ANY)
+    weight_bytes = 3 * features * hidden * 2
+    return pl.pallas_call(
+        functools.partial(fused_kernel, nz),
+        out_shape=jax.ShapeDtypeStruct(tokens.shape, kind),
+        in_specs=[vmem, vmem, vmem, hbm, hbm, hbm],
+        out_specs=vmem,
+        scratch_shapes=[
+            pltpu.VMEM((features, hidden), kind),
+            pltpu.VMEM((features, hidden), kind),
+            pltpu.VMEM((hidden, features), kind),
+            pltpu.VMEM((SQUARE, CORES, nz, rows, features + LANES), kind),
+            pltpu.VMEM((SQUARE * group, hidden), kind),
+            pltpu.VMEM((SQUARE, CORES, nz, rows, features), kind),
+            pltpu.VMEM((SQUARE, nz, rows, features), kind),
+            pltpu.VMEM((2, nz, rows, features), kind),
+            pltpu.VMEM((nz, rows, features), kind),
+            pltpu.VMEM((nz, rows, features), kind),
+            dma((3,)),
+            dma((SQUARE, CORES, nz)),
+            dma((nz,)),
+            dma((nz,)),
+            dma((2, nz)),
+            dma((SQUARE, nz)),
+            dma((SQUARE,)),
+            dma((SQUARE,)),
+            dma((2, nz)),
+            dma((2, nz)),
+            dma((nz,)),
+            dma((nz,)),
+            dma((nz,)),
+            dma((nz,)),
+        ],
+        compiler_params=pltpu.CompilerParams(
+            collective_id=0, has_side_effects=True, vmem_limit_bytes=56 * 1024 * 1024
+        ),
+        cost_estimate=pl.CostEstimate(
+            flops=2 * device_count * rows * 3 * features * hidden,
+            bytes_accessed=weight_bytes,
+            transcendentals=device_count * rows * hidden,
+        ),
+    )(tokens, expert_ids, route_weight, gate_weight, up_weight, down_weight)
+
+
 def shards(tokens, expert_ids, route_weight, gate_weight, up_weight, down_weight):
     device_count = lax.axis_size("ep")
     expert_count = device_count // 2
     tok_rows = tokens.shape[1]
     features = tokens.shape[2]
     capacity = min(tok_rows, 2 * tok_rows * TOP // expert_count)
+    every_row = capacity == tok_rows and device_count % (SQUARE * CORES) == 0
+    if every_row and STEPS * tok_rows % 16 == 0:
+        return fused(tokens, expert_ids, route_weight, gate_weight, up_weight, down_weight)
     half_slots = capacity // 2
     gate_m = gate_weight[0]
     up_m = up_weight[0]

time: 151 us -> 60.4 us (0.40)
  waiting for transfers between devices: 84.2 us -> 0 us
  Pallas kernels: 0 us -> 58.7 us
  matrix products: 20 us -> 0 us
  starting transfers between devices: 19.4 us -> 0 us
  local copies, waits for them, and re-layouts: 14.5 us -> 1.55 us
  other arithmetic: 11.4 us -> 0 us
    all_to_all x4 -> x0, waiting for transfers between devices: 84.2 us -> none  [the longest x2 42.3 us: shards(): lax.all_to_all(sent, 'ep', split_axis=0, concat_axis=0, tiled=True)]
    pallas_call x0 -> x1, Pallas kernels: none -> 58.7 us  [fused(): pl.pallas_call(functools.partial(fused_kernel, nz), out_shape=jax.ShapeDt...]
    dot_general x6 -> x0, matrix products: 20 us -> none  [the longest x2 12.8 us: shards(): jnp.einsum('scf,fd->scd', act, down_m, preferred_element_type=jnp.float32)]
    all_to_all x4 -> x0, starting transfers between devices: 18.8 us -> none  [the longest x2 11.2 us: shards(): lax.all_to_all(sent, 'ep', split_axis=0, concat_axis=0, tiled=True)]
    convert_element_type x2 -> x0, other arithmetic: 5.83 us -> none  [shards(): (parts[:, :width].astype(jnp.float32) + back.astype(jnp.float32)).astype(...]
    gather x4 -> x0, local copies, waits for them, and re-layouts: 3.89 us -> none  [the longest x2 2.24 us: shards(): padded[slot_source // TOP].reshape(expert_count, capacity, features)]
    slice x2 -> x0, local copies, waits for them, and re-layouts: 3.38 us -> none  [shards(): back = partner_2(parts[:, width:], 'ep', 0)]
    select_n x8 -> x0, other arithmetic: 3.36 us -> none  [the longest x2 2.6 us: shards(): jnp.where(parity_odd, arrange_paired[:, :, ::-1], arrange_paired)]
  transfers between devices with their start and end apart: 8 -> 0, of which waited for: 4 -> 0; matrix products, arithmetic and copies ran while one was open for 23% -> 0% of each run, Pallas kernels for 0% -> 0%
where the time goes in v2:
time: 60.4 us; the launch traced here: 60.3 us
  Pallas kernels  58.7 us (97%)
  local copies, waits for them, and re-layouts  1.55 us (3%)
    pallas_call x1, Pallas kernels, fused(): pl.pallas_call(functools.partial(fused_kernel, nz), out_shape=jax.ShapeDt...  58.7 us
    unnamed x1, local copies, waits for them, and re-layouts  1.55 us

profile of v2, /device:TPU:0, one launch (start us, length us, event | category | flops | bytes accessed | tf_op | source)
XLA Modules:
  0.0 60.3 jit_solution(12343105605111233423)
XLA Ops:
  0.0 58.7 %shard_map.64 = bf16[2,8,3584]{2,1,0:T(8,128)(2,1)} custom-call(bf16[2,8,3584]{2,1,0:T(8,128)(2,1)} %tok_ref.1, s32[2,8,8]{2,1,0:T(8,128)} %ids_ref.1, f32[2,8,8]{2,1,0:T(8,128)} %route_ref.1, bf16[1,3584,512]{2,1,0:T(8,128)(2,1)} %gate_hbm.1, bf16[1,3584,512]{2,1,0:T(8,128)(2,1)} %up_hbm.1, bf16[1,512,3584]{2,1,0:T(8,128)(2,1)} %down_hbm.1), custom_call_target="tpu_custom_call" | custom-call | flops 5637144576 | bytes 11010048 | tf_op jit(solution)/shard_map/pallas_call | solution.py:288
  58.7 1.6 %copy.8 = bf16[2,8,3584]{2,1,0:T(8,128)(2,1)} copy(bf16[2,8,3584]{2,1,0:T(8,128)(2,1)} %shard_map.64) | data formatting | bytes 229376

commit v3 on v2

--- a/solution.py
+++ b/solution.py
@@ -48,6 +48,9 @@
     at = z * low + (nz - 1 - z) * (1 - low)
     other = k + lax.div(k - at + nz, nz)
     return other * low + (nz - 1 - other) * (1 - low)
+
+
+OWN, FIRST, DIAGONAL, SECOND = 0, 2, 4, 6
 
 
 def fused_kernel(
@@ -69,15 +72,14 @@
     qx, qy = 2 * y + 1 - x, 2 * (1 - y) + x
     qa = qx * (1 - c) + qy * c
     qb = qy * (1 - c) + qx * c
-    qd = 3 - q
-    s = 1 - c
 
     def device(to_z, to_q, to_c):
         return {"ep": (to_z * SQUARE + to_q) * CORES + to_c}
 
-    sibling, along_a, along_b = device(z, q, s), device(z, qa, c), device(z, qb, c)
+    sibling, along_a, along_b = device(z, q, 1 - c), device(z, qa, c), device(z, qb, c)
     peers = [peer_at(k, z, nz) for k in range(nz - 1)]
     near = [z] + peers
+    far = near[::-1]
 
     loads = [
         pltpu.make_async_copy(gate_hbm.at[0], gate_w, w_sem.at[0]),
@@ -93,7 +95,7 @@
     for load in loads:
         load.start()
 
-    xg[q, c, z, :, :features] = (
+    xg[OWN, z, :, :features] = (
         tok_ref[...].astype(jnp.float32).reshape(rows, features).astype(jnp.bfloat16)
     )
     lane = lax.broadcasted_iota(jnp.int32, (rows, LANES), 1)
@@ -111,7 +113,7 @@
         high,
         jnp.where(lane_piece == 1, middle, jnp.where(lane_piece == 2, low, 0.0)),
     )
-    xg[q, c, z, :, features:] = pieces.astype(jnp.bfloat16)
+    xg[OWN, z, :, features:] = pieces.astype(jnp.bfloat16)
     pl.semaphore_wait(barrier, len(partners))
 
     sends = []
@@ -138,132 +140,144 @@
             device_id_type=pl.DeviceIdType.MESH,
         ).wait_recv()
 
-    def send_rows(at, send_sem, to):
-        send(xg.at[at], xg.at[at], send_sem, x_recv.at[at], to)
-
-    def rows_arrived(at):
-        arrived(xg.at[at], x_recv.at[at])
-
-    def forward_a(k):
-        at = (qa, c, near[k])
-        rows_arrived(at)
-        send_rows(at, x_send_b.at[1, k], along_b)
-        send_rows(at, x_send_s.at[1, k], sibling)
+    def send_rows(place, at, there, send_sem, to):
+        send(xg.at[place, at], xg.at[there, at], send_sem, x_recv.at[there, at], to)
+
+    def rows_arrived(place, at):
+        arrived(xg.at[place, at], x_recv.at[place, at])
+
+    def pass_own(k):
+        send_rows(OWN, near[k], FIRST, x_send_a.at[k], along_a)
+        send_rows(OWN, near[k], SECOND, x_send_b.at[0, k], along_b)
+        send_rows(OWN, near[k], OWN + 1, x_send_s.at[0, k], sibling)
+
+    def pass_first(k):
+        rows_arrived(FIRST, near[k])
+        send_rows(FIRST, near[k], DIAGONAL, x_send_b.at[1, k], along_b)
+        send_rows(FIRST, near[k], FIRST + 1, x_send_s.at[1, k], sibling)
+
+    def pass_last(place, k):
+        rows_arrived(place, near[k])
+        send_rows(place, near[k], place + 1, x_send_s.at[place // 2, k], sibling)
 
     for k in range(nz - 1):
-        send_rows((q, c, z), x_send_z.at[k], device(peers[k], q, c))
-    send_rows((q, c, z), x_send_a.at[0], along_a)
-    send_rows((q, c, z), x_send_b.at[0, 0], along_b)
-    send_rows((q, c, z), x_send_s.at[0, 0], sibling)
+        send_rows(OWN, z, OWN, x_send_z.at[k], device(peers[k], q, c))
+    pass_own(0)
+    late = []
     for k in range(1, nz):
-        at = (q, c, near[k])
-        rows_arrived(at)
-        send_rows(at, x_send_a.at[k], along_a)
-        send_rows(at, x_send_b.at[0, k], along_b)
-        send_rows(at, x_send_s.at[0, k], sibling)
-        forward_a(k - 1)
-    forward_a(nz - 1)
-
-    def experts_on(blocks):
-        def gathered():
-            return jnp.concatenate(
-                [xg[bq, bc, :, :, :features].reshape(nz * rows, features) for bq, bc in blocks],
-                axis=0,
-            )
-
-        tail = jnp.concatenate(
-            [xg[bq, bc, :, :, features:].reshape(nz * rows, LANES) for bq, bc in blocks], axis=0
-        ).astype(jnp.float32)
+        rows_arrived(OWN, near[k])
+        pass_own(k)
+        pass_first(k - 1)
+        if k >= 2:
+            pass_last(SECOND, k - 2)
+    pass_first(nz - 1)
+    if nz >= 2:
+        pass_last(SECOND, nz - 2)
+    for k in range(max(nz - 2, 0)):
+        pass_last(DIAGONAL, k)
+    late.append((SECOND, nz - 1))
+    for k in range(max(nz - 2, 0), nz):
+        late.append((DIAGONAL, k))
+
+    tiles = features // OUT_TILE
+    groups = [(0, (tiles + 1) // 2), ((tiles + 1) // 2, tiles)]
+    group_columns = [pl.ds(lo * OUT_TILE, (hi - lo) * OUT_TILE) for lo, hi in groups]
+
+    def experts_on(first, between):
+        places = pl.ds(first, SQUARE)
+        count = SQUARE * nz * rows
+        tail = xg[places, :, :, features:].reshape(count, LANES).astype(jnp.float32)
         tail_lane = lax.broadcasted_iota(jnp.int32, tail.shape, 1)
         scale = jnp.sum(
             jnp.where(lax.rem(tail_lane, experts) == expert, tail, 0.0), axis=1, keepdims=True
         )
-
-        def hidden_tile(j, carry):
-            columns = pl.ds(pl.multiple_of(j * FF_TILE, FF_TILE), FF_TILE)
-            gate = jnp.dot(gathered(), gate_w[:, columns], preferred_element_type=jnp.float32)
-            upper = jnp.dot(gathered(), up_w[:, columns], preferred_element_type=jnp.float32)
+        for tile in range(hidden // FF_TILE):
+            columns = pl.ds(tile * FF_TILE, FF_TILE)
+            inputs = xg[places, :, :, :features].reshape(count, features)
+            gate = jnp.dot(inputs, gate_w[:, columns], preferred_element_type=jnp.float32)
+            upper = jnp.dot(inputs, up_w[:, columns], preferred_element_type=jnp.float32)
             silu = gate / (1.0 + jnp.exp(-gate))
             act[:, columns] = (scale * (silu * upper)).astype(jnp.bfloat16)
-            return carry
-
-        def out_tile(j, carry):
-            columns = pl.ds(pl.multiple_of(j * OUT_TILE, OUT_TILE), OUT_TILE)
-            result = jnp.dot(
-                act[...], down_w[:, columns], preferred_element_type=jnp.float32
-            ).astype(jnp.bfloat16)
-            for number, (bq, bc) in enumerate(blocks):
-                part[bq, bc, :, :, columns] = result[
-                    number * nz * rows : (number + 1) * nz * rows
-                ].reshape(nz, rows, OUT_TILE)
-            return carry
-
-        lax.fori_loop(0, hidden // FF_TILE, hidden_tile, 0)
-        lax.fori_loop(0, features // OUT_TILE, out_tile, 0)
+            if between:
+                pass_last(*between.pop(0))
+        for number, (lo, hi) in enumerate(groups):
+            for tile in range(lo, hi):
+                columns = pl.ds(tile * OUT_TILE, OUT_TILE)
+                result = jnp.dot(
+                    act[...], down_w[:, columns], preferred_element_type=jnp.float32
+                ).astype(jnp.bfloat16)
+                part[places, :, :, columns] = result.reshape(SQUARE, nz, rows, OUT_TILE)
+                if between:
+                    pass_last(*between.pop(0))
+            columns = group_columns[number]
+            for place in (first, first + 2):
+                half = place // 2
+                send(
+                    part.at[place + 1, :, :, columns],
+                    rs.at[half, :, :, columns],
+                    rs_send.at[half, number],
+                    rs_recv.at[half, number],
+                    sibling,
+                )
+        while between:
+            pass_last(*between.pop(0))
+
+    def half_arrived(place):
+        for number, columns in enumerate(group_columns):
+            arrived(rs.at[place // 2, :, :, columns], rs_recv.at[place // 2, number])
 
     def f32(ref, *at):
         return ref[at].astype(jnp.float32)
 
-    def send_half(at):
-        send(part.at[at, s], rs.at[at], rs_send.at[at], rs_recv.at[at], sibling)
-
-    def half_arrived(at):
-        arrived(rs.at[at], rs_recv.at[at])
+    def both(place, at):
+        return f32(part, place, at) + f32(rs, place // 2, at)
+
+    def keep(place, at, value):
+        part[place, at] = value.astype(jnp.bfloat16)
 
     for k in range(nz):
-        rows_arrived((q, s, near[k]))
-        rows_arrived((qb, s, near[k]))
+        rows_arrived(OWN + 1, near[k])
+        rows_arrived(FIRST + 1, near[k])
     for load in loads:
         load.wait()
-    experts_on([(q, c), (q, s), (qa, c), (qb, s)])
-    send_half(q)
-    send_half(qb)
-    for k in range(nz):
-        for number, at in ((2, (qb, c, near[k])), (3, (qd, c, near[k]))):
-            rows_arrived(at)
-            send_rows(at, x_send_s.at[number, k], sibling)
-
-    far = [near[k] for k in range(nz - 1, -1, -1)]
-    half_arrived(q)
-    half_arrived(qa)
+    experts_on(OWN, late)
+
+    half_arrived(OWN)
+    half_arrived(FIRST)
     for k in range(nz):
         at = far[k]
-        part[qa, c, at] = (f32(part, qa, c, at) + f32(rs, qa, at)).astype(jnp.bfloat16)
-        send(part.at[qa, c, at], r1.at[0, at], r1_send.at[0, k], r1_recv.at[0, at], along_a)
+        keep(FIRST, at, both(FIRST, at))
+        send(part.at[FIRST, at], r1.at[0, at], r1_send.at[0, k], r1_recv.at[0, at], along_a)
 
     for k in range(nz):
-        rows_arrived((qa, s, near[k]))
-        rows_arrived((qd, s, near[k]))
-    experts_on([(qd, c), (qd, s), (qb, c), (qa, s)])
-    send_half(qd)
-    send_half(qa)
-    half_arrived(qd)
+        rows_arrived(SECOND + 1, near[k])
+        rows_arrived(DIAGONAL + 1, near[k])
+    experts_on(DIAGONAL, [])
+    half_arrived(DIAGONAL)
     for k in range(nz):
         at = far[k]
-        part[qd, c, at] = (f32(part, qd, c, at) + f32(rs, qd, at)).astype(jnp.bfloat16)
-        send(part.at[qd, c, at], r1.at[1, at], r1_send.at[1, k], r1_recv.at[1, at], along_a)
-    half_arrived(qb)
-
-    def sum_b(k):
+        keep(DIAGONAL, at, both(DIAGONAL, at))
+        send(part.at[DIAGONAL, at], r1.at[1, at], r1_send.at[1, k], r1_recv.at[1, at], along_a)
+    half_arrived(SECOND)
+
+    def sum_second(k):
         at = far[k]
         arrived(r1.at[1, at], r1_recv.at[1, at])
-        part[qb, c, at] = (
-            f32(part, qb, c, at) + f32(rs, qb, at) + f32(r1, 1, at)
-        ).astype(jnp.bfloat16)
-        send(part.at[qb, c, at], r2.at[at], r2_send.at[k], r2_recv.at[at], along_b)
+        keep(SECOND, at, both(SECOND, at) + f32(r1, 1, at))
+        send(part.at[SECOND, at], r2.at[at], r2_send.at[k], r2_recv.at[at], along_b)
 
     def sum_own(k):
         at = far[k]
         arrived(r1.at[0, at], r1_recv.at[0, at])
         arrived(r2.at[at], r2_recv.at[at])
-        return f32(part, q, c, at) + f32(rs, q, at) + f32(r1, 0, at) + f32(r2, at)
-
-    sum_b(0)
+        return both(OWN, at) + f32(r1, 0, at) + f32(r2, at)
+
+    sum_second(0)
     for k in range(nz - 1):
-        sum_b(k + 1)
+        sum_second(k + 1)
         at = far[k]
-        part[q, c, at] = sum_own(k).astype(jnp.bfloat16)
-        send(part.at[q, c, at], rz.at[z], rz_send.at[k], rz_recv.at[z], device(at, q, c))
+        keep(OWN, at, sum_own(k))
+        send(part.at[OWN, at], rz.at[z], rz_send.at[k], rz_recv.at[z], device(at, q, c))
     total = sum_own(nz - 1)
     for peer in peers:
         arrived(rz.at[peer], rz_recv.at[peer])
@@ -294,21 +308,21 @@
             pltpu.VMEM((features, hidden), kind),
             pltpu.VMEM((features, hidden), kind),
             pltpu.VMEM((hidden, features), kind),
-            pltpu.VMEM((SQUARE, CORES, nz, rows, features + LANES), kind),
+            pltpu.VMEM((SQUARE * CORES, nz, rows, features + LANES), kind),
             pltpu.VMEM((SQUARE * group, hidden), kind),
-            pltpu.VMEM((SQUARE, CORES, nz, rows, features), kind),
+            pltpu.VMEM((SQUARE * CORES, nz, rows, features), kind),
             pltpu.VMEM((SQUARE, nz, rows, features), kind),
             pltpu.VMEM((2, nz, rows, features), kind),
             pltpu.VMEM((nz, rows, features), kind),
             pltpu.VMEM((nz, rows, features), kind),
             dma((3,)),
-            dma((SQUARE, CORES, nz)),
+            dma((SQUARE * CORES, nz)),
             dma((nz,)),
             dma((nz,)),
             dma((2, nz)),
             dma((SQUARE, nz)),
-            dma((SQUARE,)),
-            dma((SQUARE,)),
+            dma((SQUARE, 2)),
+            dma((SQUARE, 2)),
             dma((2, nz)),
             dma((2, nz)),
             dma((nz,)),

time: 60.4 us -> 56.6 us (0.937)
  Pallas kernels: 58.7 us -> 54.9 us
    pallas_call x1, Pallas kernels: 58.7 us -> 54.9 us  [fused(): pl.pallas_call(functools.partial(fused_kernel, nz), out_shape=jax.ShapeDt...]
where the time goes in v3:
time: 56.6 us; the launch traced here: 56.5 us
  Pallas kernels  54.9 us (97%)
  local copies, waits for them, and re-layouts  1.55 us (3%)
    pallas_call x1, Pallas kernels, fused(): pl.pallas_call(functools.partial(fused_kernel, nz), out_shape=jax.ShapeDt...  54.9 us
    unnamed x1, local copies, waits for them, and re-layouts  1.55 us

profile of v3, /device:TPU:0, one launch (start us, length us, event | category | flops | bytes accessed | tf_op | source)
XLA Modules:
  0.0 56.5 jit_solution(11914067969511934083)
XLA Ops:
  0.0 54.9 %shard_map.64 = bf16[2,8,3584]{2,1,0:T(8,128)(2,1)} custom-call(bf16[2,8,3584]{2,1,0:T(8,128)(2,1)} %tok_ref.1, s32[2,8,8]{2,1,0:T(8,128)} %ids_ref.1, f32[2,8,8]{2,1,0:T(8,128)} %route_ref.1, bf16[1,3584,512]{2,1,0:T(8,128)(2,1)} %gate_hbm.1, bf16[1,3584,512]{2,1,0:T(8,128)(2,1)} %up_hbm.1, bf16[1,512,3584]{2,1,0:T(8,128)(2,1)} %down_hbm.1), custom_call_target="tpu_custom_call" | custom-call | flops 5637144576 | bytes 11010048 | tf_op jit(solution)/shard_map/pallas_call | solution.py:302
  54.9 1.6 %copy.8 = bf16[2,8,3584]{2,1,0:T(8,128)(2,1)} copy(bf16[2,8,3584]{2,1,0:T(8,128)(2,1)} %shard_map.64) | data formatting | bytes 229376

commit v4 on v3

--- a/solution.py
+++ b/solution.py
@@ -163,29 +163,26 @@
     for k in range(nz - 1):
         send_rows(OWN, z, OWN, x_send_z.at[k], device(peers[k], q, c))
     pass_own(0)
-    late = []
     for k in range(1, nz):
         rows_arrived(OWN, near[k])
         pass_own(k)
         pass_first(k - 1)
         if k >= 2:
             pass_last(SECOND, k - 2)
-    pass_first(nz - 1)
-    if nz >= 2:
-        pass_last(SECOND, nz - 2)
-    for k in range(max(nz - 2, 0)):
-        pass_last(DIAGONAL, k)
-    late.append((SECOND, nz - 1))
-    for k in range(max(nz - 2, 0), nz):
-        late.append((DIAGONAL, k))
 
     tiles = features // OUT_TILE
     groups = [(0, (tiles + 1) // 2), ((tiles + 1) // 2, tiles)]
     group_columns = [pl.ds(lo * OUT_TILE, (hi - lo) * OUT_TILE) for lo, hi in groups]
 
     def experts_on(first, between):
-        places = pl.ds(first, SQUARE)
-        count = SQUARE * nz * rows
+        between = list(between)
+
+        def aside():
+            if between:
+                between.pop(0)()
+
+        places = pl.ds(first, CORES)
+        count = CORES * nz * rows
         tail = xg[places, :, :, features:].reshape(count, LANES).astype(jnp.float32)
         tail_lane = lax.broadcasted_iota(jnp.int32, tail.shape, 1)
         scale = jnp.sum(
@@ -198,29 +195,25 @@
             upper = jnp.dot(inputs, up_w[:, columns], preferred_element_type=jnp.float32)
             silu = gate / (1.0 + jnp.exp(-gate))
             act[:, columns] = (scale * (silu * upper)).astype(jnp.bfloat16)
-            if between:
-                pass_last(*between.pop(0))
+            aside()
         for number, (lo, hi) in enumerate(groups):
             for tile in range(lo, hi):
                 columns = pl.ds(tile * OUT_TILE, OUT_TILE)
                 result = jnp.dot(
                     act[...], down_w[:, columns], preferred_element_type=jnp.float32
                 ).astype(jnp.bfloat16)
-                part[places, :, :, columns] = result.reshape(SQUARE, nz, rows, OUT_TILE)
-                if between:
-                    pass_last(*between.pop(0))
+                part[places, :, :, columns] = result.reshape(CORES, nz, rows, OUT_TILE)
+                aside()
             columns = group_columns[number]
-            for place in (first, first + 2):
-                half = place // 2
-                send(
-                    part.at[place + 1, :, :, columns],
-                    rs.at[half, :, :, columns],
-                    rs_send.at[half, number],
-                    rs_recv.at[half, number],
-                    sibling,
-                )
+            send(
+                part.at[first + 1, :, :, columns],
+                rs.at[first // 2, :, :, columns],
+                rs_send.at[first // 2, number],
+                rs_recv.at[first // 2, number],
+                sibling,
+            )
         while between:
-            pass_last(*between.pop(0))
+            aside()
 
     def half_arrived(place):
         for number, columns in enumerate(group_columns):
@@ -235,24 +228,35 @@
     def keep(place, at, value):
         part[place, at] = value.astype(jnp.bfloat16)
 
-    for k in range(nz):
-        rows_arrived(OWN + 1, near[k])
-        rows_arrived(FIRST + 1, near[k])
+    def sibling_rows(place):
+        for k in range(nz):
+            rows_arrived(place + 1, near[k])
+
+    def later(action, *at):
+        return functools.partial(action, *at)
+
+    def sum_first(k):
+        at = far[k]
+        if k == 0:
+            half_arrived(FIRST)
+        keep(FIRST, at, both(FIRST, at))
+        send(part.at[FIRST, at], r1.at[0, at], r1_send.at[0, k], r1_recv.at[0, at], along_a)
+
+    sibling_rows(OWN)
     for load in loads:
         load.wait()
-    experts_on(OWN, late)
-
+    split = max(nz - 2, 0)
+    asides = [later(pass_first, nz - 1)]
+    asides += [later(pass_last, SECOND, k) for k in range(split, nz)]
+    asides += [later(pass_last, DIAGONAL, k) for k in range(split)]
+    experts_on(OWN, asides)
+    sibling_rows(FIRST)
+    experts_on(FIRST, [later(pass_last, DIAGONAL, k) for k in range(split, nz)])
+    sibling_rows(SECOND)
+    experts_on(SECOND, [lambda: None] + [later(sum_first, k) for k in range(nz)])
+    sibling_rows(DIAGONAL)
+    experts_on(DIAGONAL, [])
     half_arrived(OWN)
-    half_arrived(FIRST)
-    for k in range(nz):
-        at = far[k]
-        keep(FIRST, at, both(FIRST, at))
-        send(part.at[FIRST, at], r1.at[0, at], r1_send.at[0, k], r1_recv.at[0, at], along_a)
-
-    for k in range(nz):
-        rows_arrived(SECOND + 1, near[k])
-        rows_arrived(DIAGONAL + 1, near[k])
-    experts_on(DIAGONAL, [])
     half_arrived(DIAGONAL)
     for k in range(nz):
         at = far[k]
@@ -309,7 +313,7 @@
             pltpu.VMEM((features, hidden), kind),
             pltpu.VMEM((hidden, features), kind),
             pltpu.VMEM((SQUARE * CORES, nz, rows, features + LANES), kind),
-            pltpu.VMEM((SQUARE * group, hidden), kind),
+            pltpu.VMEM((CORES * group, hidden), kind),
             pltpu.VMEM((SQUARE * CORES, nz, rows, features), kind),
             pltpu.VMEM((SQUARE, nz, rows, features), kind),
             pltpu.VMEM((2, nz, rows, features), kind),

time: 56.6 us -> 55.5 us (0.981)
  Pallas kernels: 54.9 us -> 53.8 us
    pallas_call x1, Pallas kernels: 54.9 us -> 53.8 us  [fused(): pl.pallas_call(functools.partial(fused_kernel, nz), out_shape=jax.ShapeDt...]
where the time goes in v4:
time: 55.5 us; the launch traced here: 55.3 us
  Pallas kernels  53.8 us (97%)
  local copies, waits for them, and re-layouts  1.55 us (3%)
    pallas_call x1, Pallas kernels, fused(): pl.pallas_call(functools.partial(fused_kernel, nz), out_shape=jax.ShapeDt...  53.8 us
    unnamed x1, local copies, waits for them, and re-layouts  1.55 us

profile of v4, /device:TPU:0, one launch (start us, length us, event | category | flops | bytes accessed | tf_op | source)
XLA Modules:
  0.0 55.3 jit_solution(10779652786640065072)
XLA Ops:
  0.0 53.8 %shard_map.64 = bf16[2,8,3584]{2,1,0:T(8,128)(2,1)} custom-call(bf16[2,8,3584]{2,1,0:T(8,128)(2,1)} %tok_ref.1, s32[2,8,8]{2,1,0:T(8,128)} %ids_ref.1, f32[2,8,8]{2,1,0:T(8,128)} %route_ref.1, bf16[1,3584,512]{2,1,0:T(8,128)(2,1)} %gate_hbm.1, bf16[1,3584,512]{2,1,0:T(8,128)(2,1)} %up_hbm.1, bf16[1,512,3584]{2,1,0:T(8,128)(2,1)} %down_hbm.1), custom_call_target="tpu_custom_call" | custom-call | flops 5637144576 | bytes 11010048 | tf_op jit(solution)/shard_map/pallas_call | solution.py:306
  53.8 1.6 %copy.8 = bf16[2,8,3584]{2,1,0:T(8,128)(2,1)} copy(bf16[2,8,3584]{2,1,0:T(8,128)(2,1)} %shard_map.64) | data formatting | bytes 229376

commit v5 on v4

--- a/solution.py
+++ b/solution.py
@@ -41,13 +41,6 @@
 CORES = 2
 FF_TILE = 256
 OUT_TILE = 512
-
-
-def peer_at(k, z, nz):
-    low = lax.div(2 * (nz - 1 - z) + 1, nz)
-    at = z * low + (nz - 1 - z) * (1 - low)
-    other = k + lax.div(k - at + nz, nz)
-    return other * low + (nz - 1 - other) * (1 - low)
 
 
 OWN, FIRST, DIAGONAL, SECOND = 0, 2, 4, 6
@@ -77,8 +70,11 @@
         return {"ep": (to_z * SQUARE + to_q) * CORES + to_c}
 
     sibling, along_a, along_b = device(z, q, 1 - c), device(z, qa, c), device(z, qb, c)
-    peers = [peer_at(k, z, nz) for k in range(nz - 1)]
-    near = [z] + peers
+    mate = z + 1 - 2 * lax.rem(z, 2)
+    across = [lax.rem(z + 2 * h, nz) for h in range(1, nz // 2)]
+    near = [z, mate]
+    for there in across:
+        near += [there, there + mate - z]
     far = near[::-1]
 
     loads = [
@@ -87,7 +83,7 @@
         pltpu.make_async_copy(down_hbm.at[0], down_w, w_sem.at[2]),
     ]
     barrier = pltpu.get_barrier_semaphore()
-    partners = [device(p, q, c) for p in peers] + [along_a, along_b, sibling]
+    partners = [device(p, q, c) for p in [mate] + across] + [along_a, along_b, sibling]
     for partner in partners:
         pl.semaphore_signal(
             barrier, inc=1, device_id=partner, device_id_type=pl.DeviceIdType.MESH
@@ -160,11 +156,14 @@
         rows_arrived(place, near[k])
         send_rows(place, near[k], place + 1, x_send_s.at[place // 2, k], sibling)
 
-    for k in range(nz - 1):
-        send_rows(OWN, z, OWN, x_send_z.at[k], device(peers[k], q, c))
+    for number, there in enumerate(across):
+        send_rows(OWN, z, OWN, x_send_z.at[2 * number], device(there, q, c))
+    send_rows(OWN, z, OWN, x_send_z.at[nz - 1], device(mate, q, c))
     pass_own(0)
     for k in range(1, nz):
         rows_arrived(OWN, near[k])
+        if k % 2 == 0:
+            send_rows(OWN, near[k], OWN, x_send_z.at[k - 1], device(mate, q, c))
         pass_own(k)
         pass_first(k - 1)
         if k >= 2:
@@ -280,12 +279,18 @@
     for k in range(nz - 1):
         sum_second(k + 1)
         at = far[k]
-        keep(OWN, at, sum_own(k))
-        send(part.at[OWN, at], rz.at[z], rz_send.at[k], rz_recv.at[z], device(at, q, c))
+        value = sum_own(k)
+        if k % 2 == 0:
+            keep(OWN, at, value)
+            send(part.at[OWN, at], rz.at[k], rz_send.at[k], rz_recv.at[k], device(mate, q, c))
+        else:
+            arrived(rz.at[k - 1], rz_recv.at[k - 1])
+            keep(OWN, at, value + f32(rz, k - 1))
+            send(part.at[OWN, at], rz.at[k], rz_send.at[k], rz_recv.at[k], device(at, q, c))
     total = sum_own(nz - 1)
-    for peer in peers:
-        arrived(rz.at[peer], rz_recv.at[peer])
-        total += f32(rz, peer)
+    for k in list(range(1, nz - 1, 2)) + [nz - 2]:
+        arrived(rz.at[k], rz_recv.at[k])
+        total += f32(rz, k)
     out_ref[...] = total.reshape(steps, tok_rows, features).astype(out_ref.dtype)
     for copy in sends:
         copy.wait_send()
@@ -351,7 +356,7 @@
     tok_rows = tokens.shape[1]
     features = tokens.shape[2]
     capacity = min(tok_rows, 2 * tok_rows * TOP // expert_count)
-    every_row = capacity == tok_rows and device_count % (SQUARE * CORES) == 0
+    every_row = capacity == tok_rows and device_count % (2 * SQUARE * CORES) == 0
     if every_row and STEPS * tok_rows % 16 == 0:
         return fused(tokens, expert_ids, route_weight, gate_weight, up_weight, down_weight)
     half_slots = capacity // 2

time: 55.5 us -> 54.7 us (0.986)
  Pallas kernels: 53.8 us -> 53 us
    pallas_call x1, Pallas kernels: 53.8 us -> 53 us  [fused(): pl.pallas_call(functools.partial(fused_kernel, nz), out_shape=jax.ShapeDt...]
where the time goes in v5:
time: 54.7 us; the launch traced here: 54.5 us
  Pallas kernels  53 us (97%)
  local copies, waits for them, and re-layouts  1.55 us (3%)
    pallas_call x1, Pallas kernels, fused(): pl.pallas_call(functools.partial(fused_kernel, nz), out_shape=jax.ShapeDt...  53 us
    unnamed x1, local copies, waits for them, and re-layouts  1.55 us

profile of v5, /device:TPU:0, one launch (start us, length us, event | category | flops | bytes accessed | tf_op | source)
XLA Modules:
  0.0 54.5 jit_solution(3890422804958080095)
XLA Ops:
  0.0 53.0 %shard_map.64 = bf16[2,8,3584]{2,1,0:T(8,128)(2,1)} custom-call(bf16[2,8,3584]{2,1,0:T(8,128)(2,1)} %tok_ref.1, s32[2,8,8]{2,1,0:T(8,128)} %ids_ref.1, f32[2,8,8]{2,1,0:T(8,128)} %route_ref.1, bf16[1,3584,512]{2,1,0:T(8,128)(2,1)} %gate_hbm.1, bf16[1,3584,512]{2,1,0:T(8,128)(2,1)} %up_hbm.1, bf16[1,512,3584]{2,1,0:T(8,128)(2,1)} %down_hbm.1), custom_call_target="tpu_custom_call" | custom-call | flops 5637144576 | bytes 11010048 | tf_op jit(solution)/shard_map/pallas_call | solution.py:311
  53.0 1.6 %copy.8 = bf16[2,8,3584]{2,1,0:T(8,128)(2,1)} copy(bf16[2,8,3584]{2,1,0:T(8,128)(2,1)} %shard_map.64) | data formatting | bytes 229376

commit v6 on v5

--- a/solution.py
+++ b/solution.py
@@ -47,8 +47,8 @@
 
 
 def fused_kernel(
-    nz, tok_ref, ids_ref, route_ref, gate_hbm, up_hbm, down_hbm, out_ref,
-    gate_w, up_w, down_w, xg, act, part, rs, r1, r2, rz,
+    nz, tok_hbm, ids_hbm, route_hbm, gate_hbm, up_hbm, down_hbm, out_ref,
+    tok_ref, ids_ref, route_ref, gate_w, up_w, down_w, xg, act, part, rs, r1, r2, rz,
     w_sem, x_recv, x_send_z, x_send_a, x_send_b, x_send_s,
     rs_send, rs_recv, r1_send, r1_recv, r2_send, r2_recv, rz_send, rz_recv,
 ):
@@ -75,12 +75,18 @@
     near = [z, mate]
     for there in across:
         near += [there, there + mate - z]
-    far = near[::-1]
+    crossings = len(across)
+    far = near[3::2] + [mate] + across + [z]
 
     loads = [
         pltpu.make_async_copy(gate_hbm.at[0], gate_w, w_sem.at[0]),
         pltpu.make_async_copy(up_hbm.at[0], up_w, w_sem.at[1]),
         pltpu.make_async_copy(down_hbm.at[0], down_w, w_sem.at[2]),
+    ]
+    fetches = [
+        pltpu.make_async_copy(tok_hbm, tok_ref, w_sem.at[3]),
+        pltpu.make_async_copy(ids_hbm, ids_ref, w_sem.at[4]),
+        pltpu.make_async_copy(route_hbm, route_ref, w_sem.at[5]),
     ]
     barrier = pltpu.get_barrier_semaphore()
     partners = [device(p, q, c) for p in [mate] + across] + [along_a, along_b, sibling]
@@ -88,8 +94,10 @@
         pl.semaphore_signal(
             barrier, inc=1, device_id=partner, device_id_type=pl.DeviceIdType.MESH
         )
-    for load in loads:
+    for load in fetches + loads:
         load.start()
+    for load in fetches:
+        load.wait()
 
     xg[OWN, z, :, :features] = (
         tok_ref[...].astype(jnp.float32).reshape(rows, features).astype(jnp.bfloat16)
@@ -222,10 +230,10 @@
         return ref[at].astype(jnp.float32)
 
     def both(place, at):
-        return f32(part, place, at) + f32(rs, place // 2, at)
+        return f32(part, place, *at) + f32(rs, place // 2, *at)
 
     def keep(place, at, value):
-        part[place, at] = value.astype(jnp.bfloat16)
+        part[place, *at] = value.astype(jnp.bfloat16)
 
     def sibling_rows(place):
         for k in range(nz):
@@ -238,7 +246,7 @@
         at = far[k]
         if k == 0:
             half_arrived(FIRST)
-        keep(FIRST, at, both(FIRST, at))
+        keep(FIRST, (at,), both(FIRST, (at,)))
         send(part.at[FIRST, at], r1.at[0, at], r1_send.at[0, k], r1_recv.at[0, at], along_a)
 
     sibling_rows(OWN)
@@ -255,43 +263,71 @@
     experts_on(SECOND, [lambda: None] + [later(sum_first, k) for k in range(nz)])
     sibling_rows(DIAGONAL)
     experts_on(DIAGONAL, [])
+    def piece(k, columns):
+        return (far[k], slice(None), columns)
+
+    def sum_diagonal(g, k):
+        at = piece(k, group_columns[g])
+        keep(DIAGONAL, at, both(DIAGONAL, at))
+        send(
+            part.at[DIAGONAL, *at], r1.at[1, *at],
+            r1_send.at[1 + g, k], r1_recv.at[1 + g, far[k]], along_a,
+        )
+
+    def sum_second(g, k):
+        at = piece(k, group_columns[g])
+        arrived(r1.at[1, *at], r1_recv.at[1 + g, far[k]])
+        keep(SECOND, at, both(SECOND, at) + f32(r1, 1, *at))
+        send(part.at[SECOND, *at], r2.at[at], r2_send.at[g, k], r2_recv.at[g, far[k]], along_b)
+
+    def sum_own(g, k):
+        at = piece(k, group_columns[g])
+        if g == 0:
+            arrived(r1.at[0, far[k]], r1_recv.at[0, far[k]])
+        arrived(r2.at[at], r2_recv.at[g, far[k]])
+        return both(OWN, at) + f32(r1, 0, *at) + f32(r2, *at)
+
+    def along_z(g, k):
+        columns = group_columns[g]
+        at = piece(k, columns)
+
+        def landed(number):
+            place = (number, slice(None), columns)
+            arrived(rz.at[place], rz_recv.at[g, number])
+            return f32(rz, *place)
+
+        value = sum_own(g, k)
+        if k == nz - 1:
+            for number in range(crossings, nz - 1):
+                value += landed(number)
+            out_ref[:, :, columns] = value.reshape(steps, tok_rows, value.shape[1]).astype(
+                out_ref.dtype
+            )
+            return
+        to = mate
+        if k > crossings:
+            value += landed(k - crossings - 1)
+            to = far[k]
+        keep(OWN, at, value)
+        send(
+            part.at[OWN, *at], rz.at[k, :, columns],
+            rz_send.at[g, k], rz_recv.at[g, k], device(to, q, c),
+        )
+
     half_arrived(OWN)
-    half_arrived(DIAGONAL)
-    for k in range(nz):
-        at = far[k]
-        keep(DIAGONAL, at, both(DIAGONAL, at))
-        send(part.at[DIAGONAL, at], r1.at[1, at], r1_send.at[1, k], r1_recv.at[1, at], along_a)
     half_arrived(SECOND)
-
-    def sum_second(k):
-        at = far[k]
-        arrived(r1.at[1, at], r1_recv.at[1, at])
-        keep(SECOND, at, both(SECOND, at) + f32(r1, 1, at))
-        send(part.at[SECOND, at], r2.at[at], r2_send.at[k], r2_recv.at[at], along_b)
-
-    def sum_own(k):
-        at = far[k]
-        arrived(r1.at[0, at], r1_recv.at[0, at])
-        arrived(r2.at[at], r2_recv.at[at])
-        return both(OWN, at) + f32(r1, 0, at) + f32(r2, at)
-
-    sum_second(0)
-    for k in range(nz - 1):
-        sum_second(k + 1)
-        at = far[k]
-        value = sum_own(k)
-        if k % 2 == 0:
-            keep(OWN, at, value)
-            send(part.at[OWN, at], rz.at[k], rz_send.at[k], rz_recv.at[k], device(mate, q, c))
-        else:
-            arrived(rz.at[k - 1], rz_recv.at[k - 1])
-            keep(OWN, at, value + f32(rz, k - 1))
-            send(part.at[OWN, at], rz.at[k], rz_send.at[k], rz_recv.at[k], device(at, q, c))
-    total = sum_own(nz - 1)
-    for k in list(range(1, nz - 1, 2)) + [nz - 2]:
-        arrived(rz.at[k], rz_recv.at[k])
-        total += f32(rz, k)
-    out_ref[...] = total.reshape(steps, tok_rows, features).astype(out_ref.dtype)
+    for g in range(len(groups)):
+        columns = group_columns[g]
+        arrived(rs.at[DIAGONAL // 2, :, :, columns], rs_recv.at[DIAGONAL // 2, g])
+        for k in range(nz):
+            sum_diagonal(g, k)
+    parts = [(g, k) for g in range(len(groups)) for k in range(nz)]
+    seconds = 0
+    for g, k in [at for at in parts if at[1] < nz - 1] + [at for at in parts if at[1] == nz - 1]:
+        while seconds < min(len(parts), g * nz + k + 2):
+            sum_second(*parts[seconds])
+            seconds += 1
+        along_z(g, k)
     for copy in sends:
         copy.wait_send()
 
@@ -311,9 +347,12 @@
     return pl.pallas_call(
         functools.partial(fused_kernel, nz),
         out_shape=jax.ShapeDtypeStruct(tokens.shape, kind),
-        in_specs=[vmem, vmem, vmem, hbm, hbm, hbm],
+        in_specs=[hbm] * 6,
         out_specs=vmem,
         scratch_shapes=[
+            pltpu.VMEM(tokens.shape, kind),
+            pltpu.VMEM(expert_ids.shape, expert_ids.dtype),
+            pltpu.VMEM(route_weight.shape, route_weight.dtype),
             pltpu.VMEM((features, hidden), kind),
             pltpu.VMEM((features, hidden), kind),
             pltpu.VMEM((hidden, features), kind),
@@ -324,7 +363,7 @@
             pltpu.VMEM((2, nz, rows, features), kind),
             pltpu.VMEM((nz, rows, features), kind),
             pltpu.VMEM((nz, rows, features), kind),
-            dma((3,)),
+            dma((6,)),
             dma((SQUARE * CORES, nz)),
             dma((nz,)),
             dma((nz,)),
@@ -332,12 +371,12 @@
             dma((SQUARE, nz)),
             dma((SQUARE, 2)),
             dma((SQUARE, 2)),
+            dma((3, nz)),
+            dma((3, nz)),
             dma((2, nz)),
             dma((2, nz)),
-            dma((nz,)),
-            dma((nz,)),
-            dma((nz,)),
-            dma((nz,)),
+            dma((2, nz)),
+            dma((2, nz)),
         ],
         compiler_params=pltpu.CompilerParams(
             collective_id=0, has_side_effects=True, vmem_limit_bytes=56 * 1024 * 1024

time: 54.7 us -> 58.4 us (1.068)
  Pallas kernels: 53 us -> 56.7 us
    pallas_call x1, Pallas kernels: 53 us -> 56.7 us  [fused(): pl.pallas_call(functools.partial(fused_kernel, nz), out_shape=jax.ShapeDt...]
where the time goes in v6:
time: 58.4 us; the launch traced here: 58.2 us
  Pallas kernels  56.7 us (97%)
  local copies, waits for them, and re-layouts  1.55 us (3%)
    pallas_call x1, Pallas kernels, fused(): pl.pallas_call(functools.partial(fused_kernel, nz), out_shape=jax.ShapeDt...  56.7 us
    unnamed x1, local copies, waits for them, and re-layouts  1.55 us

profile of v6, /device:TPU:0, one launch (start us, length us, event | category | flops | bytes accessed | tf_op | source)
XLA Modules:
  0.0 58.2 jit_solution(10031420965610161150)
XLA Ops:
  0.0 56.7 %shard_map.64 = bf16[2,8,3584]{2,1,0:T(8,128)(2,1)} custom-call(bf16[2,8,3584]{2,1,0:T(8,128)(2,1)} %tok_hbm.1, s32[2,8,8]{2,1,0:T(8,128)} %ids_hbm.1, f32[2,8,8]{2,1,0:T(8,128)} %route_hbm.1, bf16[1,3584,512]{2,1,0:T(8,128)(2,1)} %gate_hbm.1, bf16[1,3584,512]{2,1,0:T(8,128)(2,1)} %up_hbm.1, bf16[1,512,3584]{2,1,0:T(8,128)(2,1)} %down_hbm.1), custom_call_target="tpu_custom_call" | custom-call | flops 5637144576 | bytes 11010048 | tf_op jit(solution)/shard_map/pallas_call | solution.py:347
  56.7 1.6 %copy.8 = bf16[2,8,3584]{2,1,0:T(8,128)(2,1)} copy(bf16[2,8,3584]{2,1,0:T(8,128)(2,1)} %shard_map.64) | data formatting | bytes 229376

commit v7 on v5

--- a/solution.py
+++ b/solution.py
@@ -142,19 +142,30 @@
     def rows_arrived(place, at):
         arrived(xg.at[place, at], x_recv.at[place, at])
 
+    def pair(place, p):
+        return xg.at[place, pl.ds(near[2 * p] - lax.rem(z, 2), 2)]
+
+    def share(place, k):
+        if k % 2 == 1:
+            p = k // 2
+            send(
+                pair(place, p), pair(place + 1, p),
+                x_send_s.at[place // 2, p], x_recv.at[place + 1, p], sibling,
+            )
+
     def pass_own(k):
         send_rows(OWN, near[k], FIRST, x_send_a.at[k], along_a)
         send_rows(OWN, near[k], SECOND, x_send_b.at[0, k], along_b)
-        send_rows(OWN, near[k], OWN + 1, x_send_s.at[0, k], sibling)
+        share(OWN, k)
 
     def pass_first(k):
         rows_arrived(FIRST, near[k])
         send_rows(FIRST, near[k], DIAGONAL, x_send_b.at[1, k], along_b)
-        send_rows(FIRST, near[k], FIRST + 1, x_send_s.at[1, k], sibling)
+        share(FIRST, k)
 
     def pass_last(place, k):
         rows_arrived(place, near[k])
-        send_rows(place, near[k], place + 1, x_send_s.at[place // 2, k], sibling)
+        share(place, k)
 
     for number, there in enumerate(across):
         send_rows(OWN, z, OWN, x_send_z.at[2 * number], device(there, q, c))
@@ -170,7 +181,7 @@
             pass_last(SECOND, k - 2)
 
     tiles = features // OUT_TILE
-    groups = [(0, (tiles + 1) // 2), ((tiles + 1) // 2, tiles)]
+    groups = [(0, tiles)]
     group_columns = [pl.ds(lo * OUT_TILE, (hi - lo) * OUT_TILE) for lo, hi in groups]
 
     def experts_on(first, between):
@@ -228,8 +239,8 @@
         part[place, at] = value.astype(jnp.bfloat16)
 
     def sibling_rows(place):
-        for k in range(nz):
-            rows_arrived(place + 1, near[k])
+        for p in range(nz // 2):
+            arrived(pair(place + 1, p), x_recv.at[place + 1, p])
 
     def later(action, *at):
         return functools.partial(action, *at)

time: 54.7 us -> 54.7 us (level)
  no operation moved by 1% of the time
where the time goes in v7:
time: 54.7 us; the launch traced here: 54.5 us
  Pallas kernels  52.9 us (97%)
  local copies, waits for them, and re-layouts  1.55 us (3%)
    pallas_call x1, Pallas kernels, fused(): pl.pallas_call(functools.partial(fused_kernel, nz), out_shape=jax.ShapeDt...  52.9 us
    unnamed x1, local copies, waits for them, and re-layouts  1.55 us

profile of v7, /device:TPU:0, one launch (start us, length us, event | category | flops | bytes accessed | tf_op | source)
XLA Modules:
  0.0 54.5 jit_solution(3510279497594899166)
XLA Ops:
  0.0 52.9 %shard_map.64 = bf16[2,8,3584]{2,1,0:T(8,128)(2,1)} custom-call(bf16[2,8,3584]{2,1,0:T(8,128)(2,1)} %tok_ref.1, s32[2,8,8]{2,1,0:T(8,128)} %ids_ref.1, f32[2,8,8]{2,1,0:T(8,128)} %route_ref.1, bf16[1,3584,512]{2,1,0:T(8,128)(2,1)} %gate_hbm.1, bf16[1,3584,512]{2,1,0:T(8,128)(2,1)} %up_hbm.1, bf16[1,512,3584]{2,1,0:T(8,128)(2,1)} %down_hbm.1), custom_call_target="tpu_custom_call" | custom-call | flops 5637144576 | bytes 11010048 | tf_op jit(solution)/shard_map/pallas_call | solution.py:322
  52.9 1.6 %copy.8 = bf16[2,8,3584]{2,1,0:T(8,128)(2,1)} copy(bf16[2,8,3584]{2,1,0:T(8,128)(2,1)} %shard_map.64) | data formatting | bytes 229376
